TPU v7x, 256 devices: a whole 4x4x8 slice. The times are simulated.
256 devices in a mesh: ctx: 8 (over y, core), exp: 32 (over x, z).
Axes of the slice: x: 4, y: 4, z: 8, core: 2. Of those that a mesh axis runs over, the one named last changes fastest.
Arguments:
- tokens: bfloat16 [32, 1024, 2048], P('exp', 'ctx'), may hold values from -6 to 6
- input_gain: float32 [2048], replicated, may hold values from 0.1 to 1.9
- mixer_weight: bfloat16 [2048, 6144], P(None, 'ctx'), may hold values from -0.125 to 0.125
- rate_weight: bfloat16 [2048, 8, 4], P(None, 'ctx'), may hold values from -3 to 3
- conv_kernel: float32 [4, 8, 512], P(None, 'ctx'), may hold values from -3 to 3
- decay_scale: float32 [16], P('ctx'), may hold values from 0 to 0.05
- decay_bias: float32 [16], P('ctx'), may hold values from -3 to 3
- value_gain: float32 [128], replicated, may hold values from 0.1 to 1.9
- output_weight: bfloat16 [2048, 2048], P('ctx'), may hold values from -0.125 to 0.125
- start_state: float32 [16, 128, 128], P('ctx'), may hold values from -0.8 to 0.8
- post_gain: float32 [2048], replicated, may hold values from 0.1 to 1.9
- expert_gateup: bfloat16 [32, 2048, 1024], P('exp'), may hold values from -0.125 to 0.125
- expert_down: bfloat16 [32, 512, 2048], P('exp'), may hold values from -0.25 to 0.25
- route_ids: int32 [32, 1024, 4], P('exp', 'ctx'), may hold values from 0 to 31, all different within a row; in each aligned block of 128 rows (0 to 127, 128 to 255, ..., all dimensions but the last counted through in order) at most 20 rows name the same one
- route_weights: float32 [32, 1024, 4], P('exp', 'ctx'), may hold values from 0.05 to 0.5
Outputs:
- layer_out: float32 [32, 1024, 2048], P('exp', 'ctx')
- segment_states: float32 [32, 16, 128, 128], P('exp', 'ctx')
Inputs may be any that keep to these rules, and one draw needn't show every extreme that they name: `route_ids`: each token names 4 different experts. Within the 128 rows of one device (aligned blocks) no expert is named by more than 20 rows, a bound that some block reaches.
All inputs are finite; a program needn't handle non-finite values.
Results may differ from a plain program's by a relative error of at most 0.012.
Values may be sent and summed in bfloat16 or wider, within the bound.
No kernel may reach another device: no remote copies, remote signals or barrier semaphores. Data moves between devices by JAX's collectives and lax.ppermute only.
A program may use at most 128 MiB of HBM per device.

v0:
```python
import jax
import jax.numpy as jnp
from jax import lax
from jax.sharding import PartitionSpec as P

DK = 128
DV = 128
FFE = 512
KCONV = 4
HK = 8
HV = 16
BLOCK = 64
ROUTES = 4
EPSILON = 1e-06
highest = lax.Precision.HIGHEST


def passed_along(block, axis, distance):
    devices = range(lax.axis_size(axis))
    route = [(i - distance, i) for i in devices if i - distance in devices]
    return lax.ppermute(block, axis, route)


def rms_scale(values, scaling):
    widened = values.astype(jnp.float32)
    return (
        widened * lax.rsqrt(jnp.mean(widened * widened, axis=-1, keepdims=True) + EPSILON) * scaling
    )


def unit_rows(values):
    return values * lax.rsqrt(jnp.sum(values * values, axis=-1, keepdims=True) + EPSILON)


def lower_solve(strict_lower, right_side):
    result = right_side - jnp.einsum(
        "...ij,...jk->...ik", strict_lower, right_side, precision=highest
    )
    powered = strict_lower
    for _ in range((strict_lower.shape[-1] - 1).bit_length() - 1):
        powered = jnp.einsum("...ij,...jk->...ik", powered, powered, precision=highest)
        result = result + jnp.einsum("...ij,...jk->...ik", powered, result, precision=highest)
    return result


def short_conv(pre_conv, tail_rows, kernel):
    padded = jnp.concatenate([tail_rows, pre_conv], axis=0).astype(jnp.float32)
    length = pre_conv.shape[0]
    summed = jnp.zeros(pre_conv.shape, jnp.float32)
    for offset in range(kernel.shape[0]):
        summed = summed + kernel[offset] * padded[offset : offset + length]
    return jax.nn.silu(summed)


def to_blocks(array):
    moved = jnp.moveaxis(array, 1, 0)
    return moved.reshape((moved.shape[0], moved.shape[1] // BLOCK, BLOCK) + moved.shape[2:])


def head_inputs(activated, rate_rows, decay_scale, decay_bias):
    length = activated.shape[0]
    per_group = HV // HK
    head_count = activated.shape[1] * per_group
    queries = jnp.repeat(unit_rows(activated[..., :DK]) * DK ** (-0.5), per_group, axis=1)
    key_rows = jnp.repeat(unit_rows(activated[..., DK : 2 * DK]), per_group, axis=1)
    values = activated[..., 2 * DK :].reshape(length, head_count, DV)
    betas = jax.nn.sigmoid(rate_rows[..., :per_group].astype(jnp.float32)).reshape(
        length, head_count
    )
    decay_input = rate_rows[..., per_group:].astype(jnp.float32).reshape(length, head_count)
    decays = -decay_scale * jax.nn.softplus(decay_input + decay_bias)
    return (
        to_blocks(queries),
        to_blocks(key_rows),
        to_blocks(values),
        to_blocks(betas),
        to_blocks(decays),
    )


def block_terms(queries, key_rows, values, betas, decays):
    cumulative = jnp.cumsum(decays, axis=-1)
    row_index = jnp.arange(BLOCK)[:, None]
    col_index = jnp.arange(BLOCK)[None, :]
    decay_gaps = cumulative[..., :, None] - cumulative[..., None, :]
    causal = jnp.exp(jnp.where(row_index >= col_index, decay_gaps, -1e30))
    strict = jnp.where(row_index > col_index, causal, 0.0)
    key_gram = jnp.einsum("hncd,hnmd->hncm", key_rows, key_rows, precision=highest)
    strict_lower = betas[..., :, None] * key_gram * strict
    grown = jnp.exp(cumulative)[..., None]
    right_side = jnp.concatenate(
        [betas[..., None] * key_rows * grown, betas[..., None] * values], axis=-1
    )
    solved = lower_solve(strict_lower, right_side)
    wide_keys = solved[..., :DK]
    new_values = solved[..., DK:]
    scores = jnp.einsum("hncd,hnmd->hncm", queries, key_rows, precision=highest) * causal
    readers = queries * grown - jnp.einsum("hncm,hnmd->hncd", scores, wide_keys, precision=highest)
    local_out = jnp.einsum("hncm,hnme->hnce", scores, new_values, precision=highest)
    last_sum = cumulative[..., -1:]
    faded_keys = key_rows * jnp.exp(last_sum - cumulative)[..., None]
    identity = jnp.eye(DK, dtype=jnp.float32)
    transfer = jnp.exp(last_sum)[..., None] * identity - jnp.einsum(
        "hncd,hnce->hnde", faded_keys, wide_keys, precision=highest
    )
    inject = jnp.einsum("hncd,hnce->hnde", faded_keys, new_values, precision=highest)
    return (readers, local_out, transfer, inject)


def apply_state(readers, state):
    return jnp.einsum("hcd,hde->hce", readers, state, precision=highest)


def advance(transfer, state):
    return jnp.einsum("hde,hef->hdf", transfer, state, precision=highest)


def gate_norm(mixer_out, gate_part, value_gain):
    normed = (
        mixer_out
        * lax.rsqrt(jnp.mean(mixer_out * mixer_out, axis=-1, keepdims=True) + EPSILON)
        * value_gain
    )
    gated = normed * jax.nn.silu(gate_part.astype(jnp.float32))
    return gated.reshape(mixer_out.shape[0], -1).astype(jnp.bfloat16)


def body(
    tokens,
    input_gain,
    mixer_weight,
    rate_weight,
    conv_kernel,
    decay_scale,
    decay_bias,
    value_gain,
    output_weight,
    start_state,
    post_gain,
    expert_gateup,
    expert_down,
    route_ids,
    route_weights,
):
    own_rows = tokens[0]
    tok_rows = own_rows.shape[0]
    model_width = own_rows.shape[1]
    conv_width = 2 * DK + HV // HK * DV
    normed = rms_scale(own_rows, input_gain).astype(jnp.bfloat16)
    segment = lax.all_gather(normed, "ctx", axis=0, tiled=True)
    seg_rows = segment.shape[0]
    groups = rate_weight.shape[1]
    projected = (
        jnp.dot(segment, mixer_weight, preferred_element_type=jnp.float32)
        .astype(jnp.bfloat16)
        .reshape(seg_rows, groups, -1)
    )
    rate_rows = (
        jnp.dot(segment, rate_weight.reshape(model_width, -1), preferred_element_type=jnp.float32)
        .astype(jnp.bfloat16)
        .reshape(seg_rows, groups, -1)
    )
    pre_conv = projected[..., :conv_width]
    tail_rows = passed_along(pre_conv[seg_rows - (KCONV - 1) :], "exp", 1)
    activated = short_conv(pre_conv, tail_rows, conv_kernel)
    queries, key_rows, values, betas, decays = head_inputs(
        activated, rate_rows, decay_scale, decay_bias
    )
    readers, local_out, transfer, inject = block_terms(queries, key_rows, values, betas, decays)
    stacked = tuple(
        (jnp.moveaxis(member, 1, 0) for member in (readers, local_out, transfer, inject))
    )
    heads_here = readers.shape[0]
    zero_state = jnp.zeros((heads_here, DK, DV), jnp.float32)
    identity = jnp.broadcast_to(jnp.eye(DK, dtype=jnp.float32), (heads_here, DK, DK))

    def summary_step(carried, block_parts):
        partial_state, product = carried
        return (
            (
                advance(block_parts[2], partial_state) + block_parts[3],
                advance(block_parts[2], product),
            ),
            None,
        )

    (seg_inject, seg_transfer), _ = lax.scan(summary_step, (zero_state, identity), stacked)
    first_device = lax.axis_index("exp") == 0

    def relay_step(counter, arriving):
        passed = passed_along(advance(seg_transfer, arriving) + seg_inject, "exp", 1)
        return jnp.where(first_device, start_state, passed)

    incoming = lax.fori_loop(
        0, lax.axis_size("exp") - 1, relay_step, jnp.where(first_device, start_state, zero_state)
    )

    def second_step(carried, block_parts):
        out_rows = apply_state(block_parts[0], carried) + block_parts[1]
        return (advance(block_parts[2], carried) + block_parts[3], out_rows)

    final_state, outputs = lax.scan(second_step, incoming, stacked)
    mixer_out = jnp.moveaxis(outputs, 0, 1).reshape(heads_here, seg_rows, DV).transpose(1, 0, 2)
    gate_part = projected[..., conv_width:].reshape(seg_rows, heads_here, DV)
    gated = gate_norm(mixer_out, gate_part, value_gain)
    mixed = lax.psum_scatter(
        jnp.dot(gated, output_weight, preferred_element_type=jnp.float32),
        "ctx",
        scatter_dimension=0,
        tiled=True,
    )
    hidden_state = own_rows.astype(jnp.float32) + mixed
    post = rms_scale(hidden_state, post_gain).astype(jnp.bfloat16)
    expert_count = lax.axis_size("exp")
    capacity = 5 * tok_rows * ROUTES // (4 * expert_count)
    id_list = route_ids[0].reshape(-1)
    onehot = (id_list[:, None] == jnp.arange(expert_count, dtype=jnp.int32)[None, :]).astype(
        jnp.int32
    )
    slots = jnp.sum((jnp.cumsum(onehot, axis=0) - onehot) * onehot, axis=1)
    destination = id_list * capacity + slots
    token_index = jnp.arange(tok_rows * ROUTES, dtype=jnp.int32) // ROUTES
    source_row = jnp.zeros(expert_count * capacity, jnp.int32).at[destination].set(token_index)
    filled = (
        jnp.zeros(expert_count * capacity, jnp.bfloat16)
        .at[destination]
        .set(jnp.ones(tok_rows * ROUTES, jnp.bfloat16))
    )
    outgoing = (post[source_row] * filled[:, None]).reshape(expert_count, capacity, model_width)
    arrived = lax.all_to_all(outgoing, "exp", split_axis=0, concat_axis=0, tiled=True)
    flat_rows = arrived.reshape(-1, model_width)
    gate_up = jnp.dot(flat_rows, expert_gateup[0], preferred_element_type=jnp.float32)
    expert_hidden = (jax.nn.silu(gate_up[:, :FFE]) * gate_up[:, FFE:]).astype(jnp.bfloat16)
    expert_out = jnp.dot(expert_hidden, expert_down[0], preferred_element_type=jnp.float32).astype(
        jnp.bfloat16
    )
    returned = lax.all_to_all(
        expert_out.reshape(arrived.shape), "exp", split_axis=0, concat_axis=0, tiled=True
    )
    picked = returned.reshape(expert_count * capacity, model_width)[destination].reshape(
        tok_rows, ROUTES, model_width
    )
    routed = jnp.sum(route_weights[0][..., None] * picked.astype(jnp.float32), axis=1)
    layer_out = hidden_state + routed
    return (layer_out[None], final_state[None])


def solution(mesh):
    in_specs = (
        P("exp", "ctx", None),
        P(),
        P(None, "ctx"),
        P(None, "ctx", None),
        P(None, "ctx", None),
        P("ctx"),
        P("ctx"),
        P(),
        P("ctx", None),
        P("ctx", None, None),
        P(),
        P("exp", None, None),
        P("exp", None, None),
        P("exp", "ctx", None),
        P("exp", "ctx", None),
    )
    out_specs = (P("exp", "ctx", None), P("exp", "ctx", None, None))
    return jax.shard_map(body, mesh=mesh, in_specs=in_specs, out_specs=out_specs, check_vma=False)
```

profile of v0, /device:TPU:8, one launch (start us, length us, event | category | flops | bytes accessed | tf_op | source)
XLA Modules:
  0.0 751.0 jit_solution(10715073160736058607)
XLA Ops:
  13.3 34.1 %all-gather.2.cloned.1.call-done = bf16[1024,2048]{1,0:T(8,128)(2,1)} async-done(((bf16[128,2048]{1,0:T(8,128)(2,1)}), bf16[1024,2048]{1,0:T(8,128)(2,1)}) %all-gather.2.cloned.1.call-update) | async-done | bytes 4194320 | tf_op jit(solution)/shard_map/all_gather | solution.py:150
  47.4 5.7 fusion.31
  112.1 24.2 %while.37 = (s32[]{:T(128)}, f32[2,128,128]{2,1,0:T(8,128)S(1)}, f32[2,128,128]{2,1,0:T(8,128)S(1)}, f32[16,2,128,128]{3,2,1,0:T(8,128)S(1)}, f32[16,2,128,128]{3,2,1,0:T(8,128)}, /*index=5*/s32[]{:T(128)}, s32[]{:T(128)}) while((s32[]{:T(128)}, f32[2,128,128]{2,1,0:T(8,128)S(1)}, f32[2,128,128]{2,1,0:T(8,128)S(1)}, ...), condition=%wide.region_4.5_spmd.clone, body=%wide.region_3.4_spmd.clone.sunk | while | flops 100728832 | bytes 1442907 | solution.py:187
  136.3 267.1 %while.35 = (s32[]{:T(128)}, f32[2,128,128]{2,1,0:T(8,128)S(1)}, pred[]{:T(512)}, f32[2,128,128]{2,1,0:T(8,128)S(1)}, f32[2,128,128]{2,1,0:T(8,128)S(1)}, /*index=5*/f32[2,128,128]{2,1,0:T(8,128)S(1)}, s32[]{:T(128)}) while((s32[]{:T(128)}, f32[2,128,128]{2,1,0:T(8,128)S(1)}, pred[]{:T(512)}, f32[2,128,128]{2,1,0:T(8,128)S(1)}, ...), condition=%wide.region_6.7_spmd, body=%wide.region_5.6_spmd.sunk | while | flops 50397184 | bytes 1441910 | solution.py:194
  179.2 5.6 collective-permute-start
  188.5 6.1 collective-permute-start
  198.1 5.7 collective-permute-start
  214.5 5.6 collective-permute-start
  222.9 5.6 collective-permute-start
  231.4 5.6 collective-permute-start
  239.7 5.8 collective-permute-start
  249.3 6.2 collective-permute-start
  274.9 5.6 collective-permute-start
  283.3 5.6 collective-permute-start
  291.7 5.7 collective-permute-start
  300.2 6.7 collective-permute-start
  309.7 5.9 collective-permute-start
  318.4 6.5 collective-permute-start
  327.8 6.9 collective-permute-start
  338.7 6.7 collective-permute-start
  348.5 6.3 collective-permute-start
  357.7 6.8 collective-permute-start
  367.3 6.2 collective-permute-start
  376.3 6.3 collective-permute-start
  385.4 6.1 collective-permute-start
  394.4 6.5 collective-permute-start
  403.4 47.4 %while.36 = (s32[]{:T(128)}, f32[2,128,128]{2,1,0:T(8,128)S(1)}, f32[16,2,64,128]{3,2,0,1:T(8,128)}, f32[16,2,128,128]{3,2,1,0:T(8,128)S(1)}, f32[16,2,128,128]{...) while((s32[]{:T(128)}, f32[2,128,128]{2,1,0:T(8,128)S(1)}, ...), condition=%wide.region_9.10_spmd, body=%wide.region_8.9_spmd.sunk | while | flops 75546624 | bytes 1116245 | solution.py:202
  468.7 65.3 %reduce-scatter.2.cloned.1.call-done = f32[128,2048]{1,0:T(8,128)} async-done(((f32[1024,2048]{1,0:T(8,128)}), f32[128,2048]{1,0:T(8,128)}) %reduce-scatter.2.cloned.1.call-update) | async-done | bytes 1048592 | tf_op jit(solution)/shard_map/reduce_scatter | solution.py:206
  547.2 83.5 %all_to_all.10 = bf16[32,20,2048]{2,1,0:T(8,128)(2,1)} all-to-all(bf16[32,20,2048]{2,1,0:T(8,128)(2,1)S(1)} %broadcast_multiply_fusion), channel_id=1, replica_groups=mesh['ctx'=8,'exp'=32] {'exp'}, dimensions={0} | all-to-all | bytes 5242880 | tf_op jit(solution)/shard_map/all_to_all | solution.py:230
  643.1 7.2 all-to-all-start.1
  650.4 74.7 %all-to-all-done.1 = bf16[32,20,2048]{2,1,0:T(8,128)(2,1)} async-done(((bf16[32,20,2048]{2,1,0:T(8,128)(2,1)}), bf16[32,20,2048]{2,1,0:T(8,128)(2,1)}, u32[]{:S(2)}, u32[]{:S(2)}) %all-to-all-start.1) | async-done | bytes 2621472 | tf_op jit(solution)/shard_map/all_to_all | solution.py:237
  736.9 5.6 multiply_reduce_fusion
  (382 shorter events, 323.2 us)
Async XLA Ops:
  7.2 40.2 %all-gather.2.cloned.1.call-start = ((), (), s32[]{:S(2)}) async-start(), calls=%async_computation.3 | async-start | bytes 4718592 | tf_op jit(solution)/shard_map/all_gather | solution.py:150
  10.7 523.3 %reduce-scatter.2.cloned.1.call-start = ((), (), s32[]{:S(2)}) async-start(), calls=%async_computation.4 | async-start | bytes 9437184 | tf_op jit(solution)/shard_map/reduce_scatter | solution.py:206
  53.3 11.6 %collective-permute-start.1 = (bf16[3,1,512]{2,0,1:T(4,128)(2,1)S(1)}, bf16[3,1,512]{2,0,1:T(4,128)(2,1)S(1)}, u32[]{:S(2)}, u32[]{:S(2)}) collective-permute-start(bf16[3,1,512]{2,0,1:T(4,128)(2,1)S(1)} %slice.99), channel_id=1, source_target_pairs={{0,1},{1,2},{2,3},{3,4},{4,5},{5,6},{6,7},{7,8},{8,9},{9,10},{10,1... | collective-permute-start | bytes 9224 | tf_op jit(solution)/shard_map/ppermute | solution.py:21
  143.2 6.9 collective-permute-start
  150.4 6.9 collective-permute-start
  172.0 6.9 collective-permute-start
  179.2 9.0 %collective-permute-start = (f32[2,128,128]{2,1,0:T(8,128)S(1)}, f32[2,128,128]{2,1,0:T(8,128)S(1)}, u32[]{:S(2)}, u32[]{:S(2)}) collective-permute-start(f32[2,128,128]{2,1,0:T(8,128)S(1)} %convolution_add_fusion.10), channel_id=1, source_target_pairs={{0,1},{1,2},{2,3},{3,4},{4,5},{5,6},{6,7},{7,8},{8,9},{9,10},{10,1... | collective-permute-start | bytes 393224 | tf_op jit(solution)/shard_map/while/body/eval_jaxpr/ppermute | solution.py:21
  188.5 9.3 %collective-permute-start = (f32[2,128,128]{2,1,0:T(8,128)S(1)}, f32[2,128,128]{2,1,0:T(8,128)S(1)}, u32[]{:S(2)}, u32[]{:S(2)}) collective-permute-start(f32[2,128,128]{2,1,0:T(8,128)S(1)} %convolution_add_fusion.10), channel_id=1, source_target_pairs={{0,1},{1,2},{2,3},{3,4},{4,5},{5,6},{6,7},{7,8},{8,9},{9,10},{10,1... | collective-permute-start | bytes 393224 | tf_op jit(solution)/shard_map/while/body/eval_jaxpr/ppermute | solution.py:21
  198.1 8.2 %collective-permute-start = (f32[2,128,128]{2,1,0:T(8,128)S(1)}, f32[2,128,128]{2,1,0:T(8,128)S(1)}, u32[]{:S(2)}, u32[]{:S(2)}) collective-permute-start(f32[2,128,128]{2,1,0:T(8,128)S(1)} %convolution_add_fusion.10), channel_id=1, source_target_pairs={{0,1},{1,2},{2,3},{3,4},{4,5},{5,6},{6,7},{7,8},{8,9},{9,10},{10,1... | collective-permute-start | bytes 393224 | tf_op jit(solution)/shard_map/while/body/eval_jaxpr/ppermute | solution.py:21
  206.6 7.6 %collective-permute-start = (f32[2,128,128]{2,1,0:T(8,128)S(1)}, f32[2,128,128]{2,1,0:T(8,128)S(1)}, u32[]{:S(2)}, u32[]{:S(2)}) collective-permute-start(f32[2,128,128]{2,1,0:T(8,128)S(1)} %convolution_add_fusion.10), channel_id=1, source_target_pairs={{0,1},{1,2},{2,3},{3,4},{4,5},{5,6},{6,7},{7,8},{8,9},{9,10},{10,1... | collective-permute-start | bytes 393224 | tf_op jit(solution)/shard_map/while/body/eval_jaxpr/ppermute | solution.py:21
  214.5 8.1 %collective-permute-start = (f32[2,128,128]{2,1,0:T(8,128)S(1)}, f32[2,128,128]{2,1,0:T(8,128)S(1)}, u32[]{:S(2)}, u32[]{:S(2)}) collective-permute-start(f32[2,128,128]{2,1,0:T(8,128)S(1)} %convolution_add_fusion.10), channel_id=1, source_target_pairs={{0,1},{1,2},{2,3},{3,4},{4,5},{5,6},{6,7},{7,8},{8,9},{9,10},{10,1... | collective-permute-start | bytes 393224 | tf_op jit(solution)/shard_map/while/body/eval_jaxpr/ppermute | solution.py:21
  222.9 8.1 %collective-permute-start = (f32[2,128,128]{2,1,0:T(8,128)S(1)}, f32[2,128,128]{2,1,0:T(8,128)S(1)}, u32[]{:S(2)}, u32[]{:S(2)}) collective-permute-start(f32[2,128,128]{2,1,0:T(8,128)S(1)} %convolution_add_fusion.10), channel_id=1, source_target_pairs={{0,1},{1,2},{2,3},{3,4},{4,5},{5,6},{6,7},{7,8},{8,9},{9,10},{10,1... | collective-permute-start | bytes 393224 | tf_op jit(solution)/shard_map/while/body/eval_jaxpr/ppermute | solution.py:21
  231.4 8.1 %collective-permute-start = (f32[2,128,128]{2,1,0:T(8,128)S(1)}, f32[2,128,128]{2,1,0:T(8,128)S(1)}, u32[]{:S(2)}, u32[]{:S(2)}) collective-permute-start(f32[2,128,128]{2,1,0:T(8,128)S(1)} %convolution_add_fusion.10), channel_id=1, source_target_pairs={{0,1},{1,2},{2,3},{3,4},{4,5},{5,6},{6,7},{7,8},{8,9},{9,10},{10,1... | collective-permute-start | bytes 393224 | tf_op jit(solution)/shard_map/while/body/eval_jaxpr/ppermute | solution.py:21
  239.7 9.3 %collective-permute-start = (f32[2,128,128]{2,1,0:T(8,128)S(1)}, f32[2,128,128]{2,1,0:T(8,128)S(1)}, u32[]{:S(2)}, u32[]{:S(2)}) collective-permute-start(f32[2,128,128]{2,1,0:T(8,128)S(1)} %convolution_add_fusion.10), channel_id=1, source_target_pairs={{0,1},{1,2},{2,3},{3,4},{4,5},{5,6},{6,7},{7,8},{8,9},{9,10},{10,1... | collective-permute-start | bytes 393224 | tf_op jit(solution)/shard_map/while/body/eval_jaxpr/ppermute | solution.py:21
  249.3 9.2 %collective-permute-start = (f32[2,128,128]{2,1,0:T(8,128)S(1)}, f32[2,128,128]{2,1,0:T(8,128)S(1)}, u32[]{:S(2)}, u32[]{:S(2)}) collective-permute-start(f32[2,128,128]{2,1,0:T(8,128)S(1)} %convolution_add_fusion.10), channel_id=1, source_target_pairs={{0,1},{1,2},{2,3},{3,4},{4,5},{5,6},{6,7},{7,8},{8,9},{9,10},{10,1... | collective-permute-start | bytes 393224 | tf_op jit(solution)/shard_map/while/body/eval_jaxpr/ppermute | solution.py:21
  258.9 7.7 %collective-permute-start = (f32[2,128,128]{2,1,0:T(8,128)S(1)}, f32[2,128,128]{2,1,0:T(8,128)S(1)}, u32[]{:S(2)}, u32[]{:S(2)}) collective-permute-start(f32[2,128,128]{2,1,0:T(8,128)S(1)} %convolution_add_fusion.10), channel_id=1, source_target_pairs={{0,1},{1,2},{2,3},{3,4},{4,5},{5,6},{6,7},{7,8},{8,9},{9,10},{10,1... | collective-permute-start | bytes 393224 | tf_op jit(solution)/shard_map/while/body/eval_jaxpr/ppermute | solution.py:21
  266.9 7.6 %collective-permute-start = (f32[2,128,128]{2,1,0:T(8,128)S(1)}, f32[2,128,128]{2,1,0:T(8,128)S(1)}, u32[]{:S(2)}, u32[]{:S(2)}) collective-permute-start(f32[2,128,128]{2,1,0:T(8,128)S(1)} %convolution_add_fusion.10), channel_id=1, source_target_pairs={{0,1},{1,2},{2,3},{3,4},{4,5},{5,6},{6,7},{7,8},{8,9},{9,10},{10,1... | collective-permute-start | bytes 393224 | tf_op jit(solution)/shard_map/while/body/eval_jaxpr/ppermute | solution.py:21
  274.9 8.1 %collective-permute-start = (f32[2,128,128]{2,1,0:T(8,128)S(1)}, f32[2,128,128]{2,1,0:T(8,128)S(1)}, u32[]{:S(2)}, u32[]{:S(2)}) collective-permute-start(f32[2,128,128]{2,1,0:T(8,128)S(1)} %convolution_add_fusion.10), channel_id=1, source_target_pairs={{0,1},{1,2},{2,3},{3,4},{4,5},{5,6},{6,7},{7,8},{8,9},{9,10},{10,1... | collective-permute-start | bytes 393224 | tf_op jit(solution)/shard_map/while/body/eval_jaxpr/ppermute | solution.py:21
  283.3 8.1 %collective-permute-start = (f32[2,128,128]{2,1,0:T(8,128)S(1)}, f32[2,128,128]{2,1,0:T(8,128)S(1)}, u32[]{:S(2)}, u32[]{:S(2)}) collective-permute-start(f32[2,128,128]{2,1,0:T(8,128)S(1)} %convolution_add_fusion.10), channel_id=1, source_target_pairs={{0,1},{1,2},{2,3},{3,4},{4,5},{5,6},{6,7},{7,8},{8,9},{9,10},{10,1... | collective-permute-start | bytes 393224 | tf_op jit(solution)/shard_map/while/body/eval_jaxpr/ppermute | solution.py:21
  291.7 8.2 %collective-permute-start = (f32[2,128,128]{2,1,0:T(8,128)S(1)}, f32[2,128,128]{2,1,0:T(8,128)S(1)}, u32[]{:S(2)}, u32[]{:S(2)}) collective-permute-start(f32[2,128,128]{2,1,0:T(8,128)S(1)} %convolution_add_fusion.10), channel_id=1, source_target_pairs={{0,1},{1,2},{2,3},{3,4},{4,5},{5,6},{6,7},{7,8},{8,9},{9,10},{10,1... | collective-permute-start | bytes 393224 | tf_op jit(solution)/shard_map/while/body/eval_jaxpr/ppermute | solution.py:21
  300.2 9.2 %collective-permute-start = (f32[2,128,128]{2,1,0:T(8,128)S(1)}, f32[2,128,128]{2,1,0:T(8,128)S(1)}, u32[]{:S(2)}, u32[]{:S(2)}) collective-permute-start(f32[2,128,128]{2,1,0:T(8,128)S(1)} %convolution_add_fusion.10), channel_id=1, source_target_pairs={{0,1},{1,2},{2,3},{3,4},{4,5},{5,6},{6,7},{7,8},{8,9},{9,10},{10,1... | collective-permute-start | bytes 393224 | tf_op jit(solution)/shard_map/while/body/eval_jaxpr/ppermute | solution.py:21
  309.7 8.4 %collective-permute-start = (f32[2,128,128]{2,1,0:T(8,128)S(1)}, f32[2,128,128]{2,1,0:T(8,128)S(1)}, u32[]{:S(2)}, u32[]{:S(2)}) collective-permute-start(f32[2,128,128]{2,1,0:T(8,128)S(1)} %convolution_add_fusion.10), channel_id=1, source_target_pairs={{0,1},{1,2},{2,3},{3,4},{4,5},{5,6},{6,7},{7,8},{8,9},{9,10},{10,1... | collective-permute-start | bytes 393224 | tf_op jit(solution)/shard_map/while/body/eval_jaxpr/ppermute | solution.py:21
  318.4 9.0 %collective-permute-start = (f32[2,128,128]{2,1,0:T(8,128)S(1)}, f32[2,128,128]{2,1,0:T(8,128)S(1)}, u32[]{:S(2)}, u32[]{:S(2)}) collective-permute-start(f32[2,128,128]{2,1,0:T(8,128)S(1)} %convolution_add_fusion.10), channel_id=1, source_target_pairs={{0,1},{1,2},{2,3},{3,4},{4,5},{5,6},{6,7},{7,8},{8,9},{9,10},{10,1... | collective-permute-start | bytes 393224 | tf_op jit(solution)/shard_map/while/body/eval_jaxpr/ppermute | solution.py:21
  327.8 10.7 %collective-permute-start = (f32[2,128,128]{2,1,0:T(8,128)S(1)}, f32[2,128,128]{2,1,0:T(8,128)S(1)}, u32[]{:S(2)}, u32[]{:S(2)}) collective-permute-start(f32[2,128,128]{2,1,0:T(8,128)S(1)} %convolution_add_fusion.10), channel_id=1, source_target_pairs={{0,1},{1,2},{2,3},{3,4},{4,5},{5,6},{6,7},{7,8},{8,9},{9,10},{10,1... | collective-permute-start | bytes 393224 | tf_op jit(solution)/shard_map/while/body/eval_jaxpr/ppermute | solution.py:21
  338.7 9.5 %collective-permute-start = (f32[2,128,128]{2,1,0:T(8,128)S(1)}, f32[2,128,128]{2,1,0:T(8,128)S(1)}, u32[]{:S(2)}, u32[]{:S(2)}) collective-permute-start(f32[2,128,128]{2,1,0:T(8,128)S(1)} %convolution_add_fusion.10), channel_id=1, source_target_pairs={{0,1},{1,2},{2,3},{3,4},{4,5},{5,6},{6,7},{7,8},{8,9},{9,10},{10,1... | collective-permute-start | bytes 393224 | tf_op jit(solution)/shard_map/while/body/eval_jaxpr/ppermute | solution.py:21
  348.5 8.8 %collective-permute-start = (f32[2,128,128]{2,1,0:T(8,128)S(1)}, f32[2,128,128]{2,1,0:T(8,128)S(1)}, u32[]{:S(2)}, u32[]{:S(2)}) collective-permute-start(f32[2,128,128]{2,1,0:T(8,128)S(1)} %convolution_add_fusion.10), channel_id=1, source_target_pairs={{0,1},{1,2},{2,3},{3,4},{4,5},{5,6},{6,7},{7,8},{8,9},{9,10},{10,1... | collective-permute-start | bytes 393224 | tf_op jit(solution)/shard_map/while/body/eval_jaxpr/ppermute | solution.py:21
  357.7 9.3 %collective-permute-start = (f32[2,128,128]{2,1,0:T(8,128)S(1)}, f32[2,128,128]{2,1,0:T(8,128)S(1)}, u32[]{:S(2)}, u32[]{:S(2)}) collective-permute-start(f32[2,128,128]{2,1,0:T(8,128)S(1)} %convolution_add_fusion.10), channel_id=1, source_target_pairs={{0,1},{1,2},{2,3},{3,4},{4,5},{5,6},{6,7},{7,8},{8,9},{9,10},{10,1... | collective-permute-start | bytes 393224 | tf_op jit(solution)/shard_map/while/body/eval_jaxpr/ppermute | solution.py:21
  367.3 8.7 %collective-permute-start = (f32[2,128,128]{2,1,0:T(8,128)S(1)}, f32[2,128,128]{2,1,0:T(8,128)S(1)}, u32[]{:S(2)}, u32[]{:S(2)}) collective-permute-start(f32[2,128,128]{2,1,0:T(8,128)S(1)} %convolution_add_fusion.10), channel_id=1, source_target_pairs={{0,1},{1,2},{2,3},{3,4},{4,5},{5,6},{6,7},{7,8},{8,9},{9,10},{10,1... | collective-permute-start | bytes 393224 | tf_op jit(solution)/shard_map/while/body/eval_jaxpr/ppermute | solution.py:21
  376.3 8.8 %collective-permute-start = (f32[2,128,128]{2,1,0:T(8,128)S(1)}, f32[2,128,128]{2,1,0:T(8,128)S(1)}, u32[]{:S(2)}, u32[]{:S(2)}) collective-permute-start(f32[2,128,128]{2,1,0:T(8,128)S(1)} %convolution_add_fusion.10), channel_id=1, source_target_pairs={{0,1},{1,2},{2,3},{3,4},{4,5},{5,6},{6,7},{7,8},{8,9},{9,10},{10,1... | collective-permute-start | bytes 393224 | tf_op jit(solution)/shard_map/while/body/eval_jaxpr/ppermute | solution.py:21
  385.4 8.6 %collective-permute-start = (f32[2,128,128]{2,1,0:T(8,128)S(1)}, f32[2,128,128]{2,1,0:T(8,128)S(1)}, u32[]{:S(2)}, u32[]{:S(2)}) collective-permute-start(f32[2,128,128]{2,1,0:T(8,128)S(1)} %convolution_add_fusion.10), channel_id=1, source_target_pairs={{0,1},{1,2},{2,3},{3,4},{4,5},{5,6},{6,7},{7,8},{8,9},{9,10},{10,1... | collective-permute-start | bytes 393224 | tf_op jit(solution)/shard_map/while/body/eval_jaxpr/ppermute | solution.py:21
  394.4 9.0 %collective-permute-start = (f32[2,128,128]{2,1,0:T(8,128)S(1)}, f32[2,128,128]{2,1,0:T(8,128)S(1)}, u32[]{:S(2)}, u32[]{:S(2)}) collective-permute-start(f32[2,128,128]{2,1,0:T(8,128)S(1)} %convolution_add_fusion.10), channel_id=1, source_target_pairs={{0,1},{1,2},{2,3},{3,4},{4,5},{5,6},{6,7},{7,8},{8,9},{9,10},{10,1... | collective-permute-start | bytes 393224 | tf_op jit(solution)/shard_map/while/body/eval_jaxpr/ppermute | solution.py:21
  643.1 82.0 %all-to-all-start.1 = ((bf16[32,20,2048]{2,1,0:T(8,128)(2,1)}), bf16[32,20,2048]{2,1,0:T(8,128)(2,1)}, u32[]{:S(2)}, u32[]{:S(2)}) async-start(bf16[32,20,2048]{2,1,0:T(8,128)(2,1)} %reshape.235), calls=%async_computation.2 | async-start | bytes 6291456 | tf_op jit(solution)/shard_map/all_to_all | solution.py:237
  (38 other events, 407.6 us)
Sparse Core Ops, SparseCore 0:
  10.8 36.5 all-gather.1
  459.4 74.5 reduce-scatter.1
where the time goes:
time: 757 us; the launch traced here: 751 us
  waiting for transfers between devices  257 us (34%)
  starting transfers between devices  186 us (25%)
  matrix products  130 us (17%)
  blocking collectives  83.5 us (11%)
  local copies, waits for them, and re-layouts  49.8 us (7%)
  other arithmetic  27.2 us (4%)
  between operations  15.3 us (2%)
    ppermute x32, starting transfers between devices, passed_along(): return lax.ppermute(block, axis, route)  179 us
    all_to_all x1, blocking collectives, body(): lax.all_to_all(outgoing, 'exp', split_axis=0, concat_axis=0, tiled=True)  83.5 us
    ppermute x32, waiting for transfers between devices, passed_along(): return lax.ppermute(block, axis, route)  82.5 us
    all_to_all x1, waiting for transfers between devices, body(): lax.all_to_all(expert_out.reshape(arrived.shape), 'exp', split_axis=0, co...  74.7 us
    reduce_scatter x1, waiting for transfers between devices, body(): lax.psum_scatter(jnp.dot(gated, output_weight, preferred_element_type=jnp...  65.3 us
    dot_general x79, matrix products, advance(): return jnp.einsum('hde,hef->hdf', transfer, state, precision=highest)  50 us
    all_gather x1, waiting for transfers between devices, body(): segment = lax.all_gather(normed, 'ctx', axis=0, tiled=True)  34.1 us
    dot_general x16, matrix products, apply_state(): return jnp.einsum('hcd,hde->hce', readers, state, precision=highest)  28 us
  transfers between devices with their start and end apart: 35, of which 34 were waited for; matrix products, arithmetic and copies ran while one was open for 3% of the time, Pallas kernels for 0%

commit v1 on v0

--- a/solution.py
+++ b/solution.py
@@ -147,7 +147,9 @@
     model_width = own_rows.shape[1]
     conv_width = 2 * DK + HV // HK * DV
     normed = rms_scale(own_rows, input_gain).astype(jnp.bfloat16)
-    segment = lax.all_gather(normed, "ctx", axis=0, tiled=True)
+    segment = jnp.concatenate(
+        lax.all_to_all(jnp.stack([normed] * lax.axis_size("ctx")), "ctx", 0, 0), axis=0
+    )
     seg_rows = segment.shape[0]
     groups = rate_weight.shape[1]
     projected = (

time: 757 us -> 777 us (1.026)
  waiting for transfers between devices: 257 us -> 268 us
    all_to_all x0 -> x1, waiting for transfers between devices: none -> 46.4 us  [body(): lax.all_to_all(jnp.stack([normed] * lax.axis_size('ctx')), 'ctx', 0, 0)]
    all_gather x1 -> x0, waiting for transfers between devices: 34.1 us -> none  [body(): segment = lax.all_gather(normed, 'ctx', axis=0, tiled=True)]
where the time goes in v1:
time: 777 us; the launch traced here: 771 us
  waiting for transfers between devices  268 us (34%)
  starting transfers between devices  191 us (25%)
  matrix products  132 us (17%)
  blocking collectives  83.4 us (11%)
  local copies, waits for them, and re-layouts  52.2 us (7%)
  other arithmetic  25.8 us (3%)
  between operations  15.2 us (2%)
    ppermute x32, starting transfers between devices, passed_along(): return lax.ppermute(block, axis, route)  177 us
    all_to_all x1, blocking collectives, body(): lax.all_to_all(outgoing, 'exp', split_axis=0, concat_axis=0, tiled=True)  83.4 us
    ppermute x32, waiting for transfers between devices, passed_along(): return lax.ppermute(block, axis, route)  82.4 us
    all_to_all x1, waiting for transfers between devices, body(): lax.all_to_all(expert_out.reshape(arrived.shape), 'exp', split_axis=0, co...  74.7 us
    reduce_scatter x1, waiting for transfers between devices, body(): lax.psum_scatter(jnp.dot(gated, output_weight, preferred_element_type=jnp...  64.9 us
    dot_general x79, matrix products, advance(): return jnp.einsum('hde,hef->hdf', transfer, state, precision=highest)  50 us
    all_to_all x1, waiting for transfers between devices, body(): lax.all_to_all(jnp.stack([normed] * lax.axis_size('ctx')), 'ctx', 0, 0)  46.4 us
    dot_general x16, matrix products, apply_state(): return jnp.einsum('hcd,hde->hce', readers, state, precision=highest)  27.8 us
  transfers between devices with their start and end apart: 35, of which 34 were waited for; matrix products, arithmetic and copies ran while one was open for 3% of the time, Pallas kernels for 0%

profile of v1, /device:TPU:8, one launch (start us, length us, event | category | flops | bytes accessed | tf_op | source)
XLA Modules:
  0.0 770.6 jit_solution(766820020567078583)
XLA Ops:
  12.3 6.7 all-to-all-start
  21.0 46.4 %all-to-all-done = bf16[8,128,2048]{2,1,0:T(8,128)(2,1)} async-done(((bf16[8,128,2048]{2,1,0:T(8,128)(2,1)}), bf16[8,128,2048]{2,1,0:T(8,128)(2,1)}, u32[]{:S(2)}, u32[]{:S(2)}) %all-to-all-start) | async-done | bytes 4194336 | tf_op jit(solution)/shard_map/all_to_all | solution.py:151
  67.4 5.6 fusion.31
  132.8 24.2 %while.37 = (s32[]{:T(128)}, f32[2,128,128]{2,1,0:T(8,128)S(1)}, f32[2,128,128]{2,1,0:T(8,128)S(1)}, f32[16,2,128,128]{3,2,1,0:T(8,128)S(1)}, f32[16,2,128,128]{3,2,1,0:T(8,128)}, /*index=5*/s32[]{:T(128)}, s32[]{:T(128)}) while((s32[]{:T(128)}, f32[2,128,128]{2,1,0:T(8,128)S(1)}, f32[2,128,128]{2,1,0:T(8,128)S(1)}, ...), condition=%wide.region_4.5_spmd.clone, body=%wide.region_3.4_spmd.clone.sunk | while | flops 100728832 | bytes 1442907 | solution.py:189
  157.0 266.8 %while.35 = (s32[]{:T(128)}, f32[2,128,128]{2,1,0:T(8,128)S(1)}, pred[]{:T(512)}, f32[2,128,128]{2,1,0:T(8,128)S(1)}, f32[2,128,128]{2,1,0:T(8,128)S(1)}, /*index=5*/f32[2,128,128]{2,1,0:T(8,128)S(1)}, s32[]{:T(128)}) while((s32[]{:T(128)}, f32[2,128,128]{2,1,0:T(8,128)S(1)}, pred[]{:T(512)}, f32[2,128,128]{2,1,0:T(8,128)S(1)}, ...), condition=%wide.region_6.7_spmd, body=%wide.region_5.6_spmd.sunk | while | flops 50397184 | bytes 1441910 | solution.py:196
  201.5 5.9 collective-permute-start
  211.2 5.9 collective-permute-start
  228.1 5.6 collective-permute-start
  236.5 5.6 collective-permute-start
  244.9 5.6 collective-permute-start
  262.6 6.1 collective-permute-start
  272.2 5.8 collective-permute-start
  288.7 5.6 collective-permute-start
  297.1 5.6 collective-permute-start
  305.5 5.6 collective-permute-start
  313.9 5.6 collective-permute-start
  322.3 5.6 collective-permute-start
  339.0 6.3 collective-permute-start
  348.3 6.9 collective-permute-start
  359.3 6.4 collective-permute-start
  368.8 6.5 collective-permute-start
  378.1 6.7 collective-permute-start
  387.6 6.2 collective-permute-start
  396.6 6.3 collective-permute-start
  405.7 6.2 collective-permute-start
  414.8 6.5 collective-permute-start
  423.8 47.2 %while.36 = (s32[]{:T(128)}, f32[2,128,128]{2,1,0:T(8,128)S(1)}, f32[16,2,64,128]{3,2,0,1:T(8,128)}, f32[16,2,128,128]{3,2,1,0:T(8,128)S(1)}, f32[16,2,128,128]{...) while((s32[]{:T(128)}, f32[2,128,128]{2,1,0:T(8,128)S(1)}, ...), condition=%wide.region_9.10_spmd, body=%wide.region_8.9_spmd.sunk | while | flops 75546624 | bytes 1116245 | solution.py:204
  488.9 64.9 %reduce-scatter.2.cloned.1.call-done = f32[128,2048]{1,0:T(8,128)} async-done(((f32[1024,2048]{1,0:T(8,128)}), f32[128,2048]{1,0:T(8,128)}) %reduce-scatter.2.cloned.1.call-update) | async-done | bytes 1048592 | tf_op jit(solution)/shard_map/reduce_scatter | solution.py:208
  566.9 83.4 %all_to_all.15 = bf16[32,20,2048]{2,1,0:T(8,128)(2,1)} all-to-all(bf16[32,20,2048]{2,1,0:T(8,128)(2,1)S(1)} %broadcast_multiply_fusion), channel_id=1, replica_groups=mesh['ctx'=8,'exp'=32] {'exp'}, dimensions={0} | all-to-all | bytes 5242880 | tf_op jit(solution)/shard_map/all_to_all | solution.py:232
  662.7 7.2 all-to-all-start.2
  670.1 74.7 %all-to-all-done.2 = bf16[32,20,2048]{2,1,0:T(8,128)(2,1)} async-done(((bf16[32,20,2048]{2,1,0:T(8,128)(2,1)}), bf16[32,20,2048]{2,1,0:T(8,128)(2,1)}, u32[]{:S(2)}, u32[]{:S(2)}) %all-to-all-start.2) | async-done | bytes 2621472 | tf_op jit(solution)/shard_map/all_to_all | solution.py:239
  756.5 5.6 multiply_reduce_fusion
  (378 shorter events, 332.2 us)
Async XLA Ops:
  12.3 55.1 %all-to-all-start = ((bf16[8,128,2048]{2,1,0:T(8,128)(2,1)}), bf16[8,128,2048]{2,1,0:T(8,128)(2,1)}, u32[]{:S(2)}, u32[]{:S(2)}) async-start(bf16[8,128,2048]{2,1,0:T(8,128)(2,1)} %stack.5), calls=%async_computation | async-start | bytes 8388608 | tf_op jit(solution)/shard_map/all_to_all | solution.py:151
  19.1 534.7 %reduce-scatter.2.cloned.1.call-start = ((), (), s32[]{:S(2)}) async-start(), calls=%async_computation.4 | async-start | bytes 9437184 | tf_op jit(solution)/shard_map/reduce_scatter | solution.py:208
  73.2 12.4 %collective-permute-start.1 = (bf16[3,1,512]{2,0,1:T(4,128)(2,1)S(1)}, bf16[3,1,512]{2,0,1:T(4,128)(2,1)S(1)}, u32[]{:S(2)}, u32[]{:S(2)}) collective-permute-start(bf16[3,1,512]{2,0,1:T(4,128)(2,1)S(1)} %slice.99), channel_id=1, source_target_pairs={{0,1},{1,2},{2,3},{3,4},{4,5},{5,6},{6,7},{7,8},{8,9},{9,10},{10,1... | collective-permute-start | bytes 9224 | tf_op jit(solution)/shard_map/ppermute | solution.py:21
  163.9 6.9 collective-permute-start
  171.1 7.0 collective-permute-start
  192.7 8.5 %collective-permute-start = (f32[2,128,128]{2,1,0:T(8,128)S(1)}, f32[2,128,128]{2,1,0:T(8,128)S(1)}, u32[]{:S(2)}, u32[]{:S(2)}) collective-permute-start(f32[2,128,128]{2,1,0:T(8,128)S(1)} %convolution_add_fusion.10), channel_id=1, source_target_pairs={{0,1},{1,2},{2,3},{3,4},{4,5},{5,6},{6,7},{7,8},{8,9},{9,10},{10,1... | collective-permute-start | bytes 393224 | tf_op jit(solution)/shard_map/while/body/eval_jaxpr/ppermute | solution.py:21
  201.5 9.3 %collective-permute-start = (f32[2,128,128]{2,1,0:T(8,128)S(1)}, f32[2,128,128]{2,1,0:T(8,128)S(1)}, u32[]{:S(2)}, u32[]{:S(2)}) collective-permute-start(f32[2,128,128]{2,1,0:T(8,128)S(1)} %convolution_add_fusion.10), channel_id=1, source_target_pairs={{0,1},{1,2},{2,3},{3,4},{4,5},{5,6},{6,7},{7,8},{8,9},{9,10},{10,1... | collective-permute-start | bytes 393224 | tf_op jit(solution)/shard_map/while/body/eval_jaxpr/ppermute | solution.py:21
  211.2 8.4 %collective-permute-start = (f32[2,128,128]{2,1,0:T(8,128)S(1)}, f32[2,128,128]{2,1,0:T(8,128)S(1)}, u32[]{:S(2)}, u32[]{:S(2)}) collective-permute-start(f32[2,128,128]{2,1,0:T(8,128)S(1)} %convolution_add_fusion.10), channel_id=1, source_target_pairs={{0,1},{1,2},{2,3},{3,4},{4,5},{5,6},{6,7},{7,8},{8,9},{9,10},{10,1... | collective-permute-start | bytes 393224 | tf_op jit(solution)/shard_map/while/body/eval_jaxpr/ppermute | solution.py:21
  219.9 7.9 %collective-permute-start = (f32[2,128,128]{2,1,0:T(8,128)S(1)}, f32[2,128,128]{2,1,0:T(8,128)S(1)}, u32[]{:S(2)}, u32[]{:S(2)}) collective-permute-start(f32[2,128,128]{2,1,0:T(8,128)S(1)} %convolution_add_fusion.10), channel_id=1, source_target_pairs={{0,1},{1,2},{2,3},{3,4},{4,5},{5,6},{6,7},{7,8},{8,9},{9,10},{10,1... | collective-permute-start | bytes 393224 | tf_op jit(solution)/shard_map/while/body/eval_jaxpr/ppermute | solution.py:21
  228.1 8.1 %collective-permute-start = (f32[2,128,128]{2,1,0:T(8,128)S(1)}, f32[2,128,128]{2,1,0:T(8,128)S(1)}, u32[]{:S(2)}, u32[]{:S(2)}) collective-permute-start(f32[2,128,128]{2,1,0:T(8,128)S(1)} %convolution_add_fusion.10), channel_id=1, source_target_pairs={{0,1},{1,2},{2,3},{3,4},{4,5},{5,6},{6,7},{7,8},{8,9},{9,10},{10,1... | collective-permute-start | bytes 393224 | tf_op jit(solution)/shard_map/while/body/eval_jaxpr/ppermute | solution.py:21
  236.5 8.1 %collective-permute-start = (f32[2,128,128]{2,1,0:T(8,128)S(1)}, f32[2,128,128]{2,1,0:T(8,128)S(1)}, u32[]{:S(2)}, u32[]{:S(2)}) collective-permute-start(f32[2,128,128]{2,1,0:T(8,128)S(1)} %convolution_add_fusion.10), channel_id=1, source_target_pairs={{0,1},{1,2},{2,3},{3,4},{4,5},{5,6},{6,7},{7,8},{8,9},{9,10},{10,1... | collective-permute-start | bytes 393224 | tf_op jit(solution)/shard_map/while/body/eval_jaxpr/ppermute | solution.py:21
  244.9 8.1 %collective-permute-start = (f32[2,128,128]{2,1,0:T(8,128)S(1)}, f32[2,128,128]{2,1,0:T(8,128)S(1)}, u32[]{:S(2)}, u32[]{:S(2)}) collective-permute-start(f32[2,128,128]{2,1,0:T(8,128)S(1)} %convolution_add_fusion.10), channel_id=1, source_target_pairs={{0,1},{1,2},{2,3},{3,4},{4,5},{5,6},{6,7},{7,8},{8,9},{9,10},{10,1... | collective-permute-start | bytes 393224 | tf_op jit(solution)/shard_map/while/body/eval_jaxpr/ppermute | solution.py:21
  253.3 9.0 %collective-permute-start = (f32[2,128,128]{2,1,0:T(8,128)S(1)}, f32[2,128,128]{2,1,0:T(8,128)S(1)}, u32[]{:S(2)}, u32[]{:S(2)}) collective-permute-start(f32[2,128,128]{2,1,0:T(8,128)S(1)} %convolution_add_fusion.10), channel_id=1, source_target_pairs={{0,1},{1,2},{2,3},{3,4},{4,5},{5,6},{6,7},{7,8},{8,9},{9,10},{10,1... | collective-permute-start | bytes 393224 | tf_op jit(solution)/shard_map/while/body/eval_jaxpr/ppermute | solution.py:21
  262.6 9.3 %collective-permute-start = (f32[2,128,128]{2,1,0:T(8,128)S(1)}, f32[2,128,128]{2,1,0:T(8,128)S(1)}, u32[]{:S(2)}, u32[]{:S(2)}) collective-permute-start(f32[2,128,128]{2,1,0:T(8,128)S(1)} %convolution_add_fusion.10), channel_id=1, source_target_pairs={{0,1},{1,2},{2,3},{3,4},{4,5},{5,6},{6,7},{7,8},{8,9},{9,10},{10,1... | collective-permute-start | bytes 393224 | tf_op jit(solution)/shard_map/while/body/eval_jaxpr/ppermute | solution.py:21
  272.2 8.3 %collective-permute-start = (f32[2,128,128]{2,1,0:T(8,128)S(1)}, f32[2,128,128]{2,1,0:T(8,128)S(1)}, u32[]{:S(2)}, u32[]{:S(2)}) collective-permute-start(f32[2,128,128]{2,1,0:T(8,128)S(1)} %convolution_add_fusion.10), channel_id=1, source_target_pairs={{0,1},{1,2},{2,3},{3,4},{4,5},{5,6},{6,7},{7,8},{8,9},{9,10},{10,1... | collective-permute-start | bytes 393224 | tf_op jit(solution)/shard_map/while/body/eval_jaxpr/ppermute | solution.py:21
  280.8 7.6 collective-permute-start
  288.7 8.1 %collective-permute-start = (f32[2,128,128]{2,1,0:T(8,128)S(1)}, f32[2,128,128]{2,1,0:T(8,128)S(1)}, u32[]{:S(2)}, u32[]{:S(2)}) collective-permute-start(f32[2,128,128]{2,1,0:T(8,128)S(1)} %convolution_add_fusion.10), channel_id=1, source_target_pairs={{0,1},{1,2},{2,3},{3,4},{4,5},{5,6},{6,7},{7,8},{8,9},{9,10},{10,1... | collective-permute-start | bytes 393224 | tf_op jit(solution)/shard_map/while/body/eval_jaxpr/ppermute | solution.py:21
  297.1 8.1 %collective-permute-start = (f32[2,128,128]{2,1,0:T(8,128)S(1)}, f32[2,128,128]{2,1,0:T(8,128)S(1)}, u32[]{:S(2)}, u32[]{:S(2)}) collective-permute-start(f32[2,128,128]{2,1,0:T(8,128)S(1)} %convolution_add_fusion.10), channel_id=1, source_target_pairs={{0,1},{1,2},{2,3},{3,4},{4,5},{5,6},{6,7},{7,8},{8,9},{9,10},{10,1... | collective-permute-start | bytes 393224 | tf_op jit(solution)/shard_map/while/body/eval_jaxpr/ppermute | solution.py:21
  305.5 8.1 %collective-permute-start = (f32[2,128,128]{2,1,0:T(8,128)S(1)}, f32[2,128,128]{2,1,0:T(8,128)S(1)}, u32[]{:S(2)}, u32[]{:S(2)}) collective-permute-start(f32[2,128,128]{2,1,0:T(8,128)S(1)} %convolution_add_fusion.10), channel_id=1, source_target_pairs={{0,1},{1,2},{2,3},{3,4},{4,5},{5,6},{6,7},{7,8},{8,9},{9,10},{10,1... | collective-permute-start | bytes 393224 | tf_op jit(solution)/shard_map/while/body/eval_jaxpr/ppermute | solution.py:21
  313.9 8.1 %collective-permute-start = (f32[2,128,128]{2,1,0:T(8,128)S(1)}, f32[2,128,128]{2,1,0:T(8,128)S(1)}, u32[]{:S(2)}, u32[]{:S(2)}) collective-permute-start(f32[2,128,128]{2,1,0:T(8,128)S(1)} %convolution_add_fusion.10), channel_id=1, source_target_pairs={{0,1},{1,2},{2,3},{3,4},{4,5},{5,6},{6,7},{7,8},{8,9},{9,10},{10,1... | collective-permute-start | bytes 393224 | tf_op jit(solution)/shard_map/while/body/eval_jaxpr/ppermute | solution.py:21
  322.3 8.1 %collective-permute-start = (f32[2,128,128]{2,1,0:T(8,128)S(1)}, f32[2,128,128]{2,1,0:T(8,128)S(1)}, u32[]{:S(2)}, u32[]{:S(2)}) collective-permute-start(f32[2,128,128]{2,1,0:T(8,128)S(1)} %convolution_add_fusion.10), channel_id=1, source_target_pairs={{0,1},{1,2},{2,3},{3,4},{4,5},{5,6},{6,7},{7,8},{8,9},{9,10},{10,1... | collective-permute-start | bytes 393224 | tf_op jit(solution)/shard_map/while/body/eval_jaxpr/ppermute | solution.py:21
  330.7 8.1 %collective-permute-start = (f32[2,128,128]{2,1,0:T(8,128)S(1)}, f32[2,128,128]{2,1,0:T(8,128)S(1)}, u32[]{:S(2)}, u32[]{:S(2)}) collective-permute-start(f32[2,128,128]{2,1,0:T(8,128)S(1)} %convolution_add_fusion.10), channel_id=1, source_target_pairs={{0,1},{1,2},{2,3},{3,4},{4,5},{5,6},{6,7},{7,8},{8,9},{9,10},{10,1... | collective-permute-start | bytes 393224 | tf_op jit(solution)/shard_map/while/body/eval_jaxpr/ppermute | solution.py:21
  339.0 8.9 %collective-permute-start = (f32[2,128,128]{2,1,0:T(8,128)S(1)}, f32[2,128,128]{2,1,0:T(8,128)S(1)}, u32[]{:S(2)}, u32[]{:S(2)}) collective-permute-start(f32[2,128,128]{2,1,0:T(8,128)S(1)} %convolution_add_fusion.10), channel_id=1, source_target_pairs={{0,1},{1,2},{2,3},{3,4},{4,5},{5,6},{6,7},{7,8},{8,9},{9,10},{10,1... | collective-permute-start | bytes 393224 | tf_op jit(solution)/shard_map/while/body/eval_jaxpr/ppermute | solution.py:21
  348.3 10.7 %collective-permute-start = (f32[2,128,128]{2,1,0:T(8,128)S(1)}, f32[2,128,128]{2,1,0:T(8,128)S(1)}, u32[]{:S(2)}, u32[]{:S(2)}) collective-permute-start(f32[2,128,128]{2,1,0:T(8,128)S(1)} %convolution_add_fusion.10), channel_id=1, source_target_pairs={{0,1},{1,2},{2,3},{3,4},{4,5},{5,6},{6,7},{7,8},{8,9},{9,10},{10,1... | collective-permute-start | bytes 393224 | tf_op jit(solution)/shard_map/while/body/eval_jaxpr/ppermute | solution.py:21
  359.3 9.2 %collective-permute-start = (f32[2,128,128]{2,1,0:T(8,128)S(1)}, f32[2,128,128]{2,1,0:T(8,128)S(1)}, u32[]{:S(2)}, u32[]{:S(2)}) collective-permute-start(f32[2,128,128]{2,1,0:T(8,128)S(1)} %convolution_add_fusion.10), channel_id=1, source_target_pairs={{0,1},{1,2},{2,3},{3,4},{4,5},{5,6},{6,7},{7,8},{8,9},{9,10},{10,1... | collective-permute-start | bytes 393224 | tf_op jit(solution)/shard_map/while/body/eval_jaxpr/ppermute | solution.py:21
  368.8 9.0 %collective-permute-start = (f32[2,128,128]{2,1,0:T(8,128)S(1)}, f32[2,128,128]{2,1,0:T(8,128)S(1)}, u32[]{:S(2)}, u32[]{:S(2)}) collective-permute-start(f32[2,128,128]{2,1,0:T(8,128)S(1)} %convolution_add_fusion.10), channel_id=1, source_target_pairs={{0,1},{1,2},{2,3},{3,4},{4,5},{5,6},{6,7},{7,8},{8,9},{9,10},{10,1... | collective-permute-start | bytes 393224 | tf_op jit(solution)/shard_map/while/body/eval_jaxpr/ppermute | solution.py:21
  378.1 9.2 %collective-permute-start = (f32[2,128,128]{2,1,0:T(8,128)S(1)}, f32[2,128,128]{2,1,0:T(8,128)S(1)}, u32[]{:S(2)}, u32[]{:S(2)}) collective-permute-start(f32[2,128,128]{2,1,0:T(8,128)S(1)} %convolution_add_fusion.10), channel_id=1, source_target_pairs={{0,1},{1,2},{2,3},{3,4},{4,5},{5,6},{6,7},{7,8},{8,9},{9,10},{10,1... | collective-permute-start | bytes 393224 | tf_op jit(solution)/shard_map/while/body/eval_jaxpr/ppermute | solution.py:21
  387.6 8.7 %collective-permute-start = (f32[2,128,128]{2,1,0:T(8,128)S(1)}, f32[2,128,128]{2,1,0:T(8,128)S(1)}, u32[]{:S(2)}, u32[]{:S(2)}) collective-permute-start(f32[2,128,128]{2,1,0:T(8,128)S(1)} %convolution_add_fusion.10), channel_id=1, source_target_pairs={{0,1},{1,2},{2,3},{3,4},{4,5},{5,6},{6,7},{7,8},{8,9},{9,10},{10,1... | collective-permute-start | bytes 393224 | tf_op jit(solution)/shard_map/while/body/eval_jaxpr/ppermute | solution.py:21
  396.6 8.8 %collective-permute-start = (f32[2,128,128]{2,1,0:T(8,128)S(1)}, f32[2,128,128]{2,1,0:T(8,128)S(1)}, u32[]{:S(2)}, u32[]{:S(2)}) collective-permute-start(f32[2,128,128]{2,1,0:T(8,128)S(1)} %convolution_add_fusion.10), channel_id=1, source_target_pairs={{0,1},{1,2},{2,3},{3,4},{4,5},{5,6},{6,7},{7,8},{8,9},{9,10},{10,1... | collective-permute-start | bytes 393224 | tf_op jit(solution)/shard_map/while/body/eval_jaxpr/ppermute | solution.py:21
  405.7 8.7 %collective-permute-start = (f32[2,128,128]{2,1,0:T(8,128)S(1)}, f32[2,128,128]{2,1,0:T(8,128)S(1)}, u32[]{:S(2)}, u32[]{:S(2)}) collective-permute-start(f32[2,128,128]{2,1,0:T(8,128)S(1)} %convolution_add_fusion.10), channel_id=1, source_target_pairs={{0,1},{1,2},{2,3},{3,4},{4,5},{5,6},{6,7},{7,8},{8,9},{9,10},{10,1... | collective-permute-start | bytes 393224 | tf_op jit(solution)/shard_map/while/body/eval_jaxpr/ppermute | solution.py:21
  414.8 9.0 %collective-permute-start = (f32[2,128,128]{2,1,0:T(8,128)S(1)}, f32[2,128,128]{2,1,0:T(8,128)S(1)}, u32[]{:S(2)}, u32[]{:S(2)}) collective-permute-start(f32[2,128,128]{2,1,0:T(8,128)S(1)} %convolution_add_fusion.10), channel_id=1, source_target_pairs={{0,1},{1,2},{2,3},{3,4},{4,5},{5,6},{6,7},{7,8},{8,9},{9,10},{10,1... | collective-permute-start | bytes 393224 | tf_op jit(solution)/shard_map/while/body/eval_jaxpr/ppermute | solution.py:21
  662.7 82.1 %all-to-all-start.2 = ((bf16[32,20,2048]{2,1,0:T(8,128)(2,1)}), bf16[32,20,2048]{2,1,0:T(8,128)(2,1)}, u32[]{:S(2)}, u32[]{:S(2)}) async-start(bf16[32,20,2048]{2,1,0:T(8,128)(2,1)} %reshape.253), calls=%async_computation.3 | async-start | bytes 6291456 | tf_op jit(solution)/shard_map/all_to_all | solution.py:239
  (36 other events, 386.2 us)
Sparse Core Ops, SparseCore 0:
  479.6 74.1 reduce-scatter.1
